TPU v7x, 32 devices: a whole 2x2x4 slice. The times are simulated.
32 devices in a mesh: gx: 2 (over x), gy: 4 (over z), gz: 4 (over y, core).
Axes of the slice: x: 2, y: 2, z: 4, core: 2. Of those that a mesh axis runs over, the one named last changes fastest.
Arguments:
- u_start: float32 [8, 256, 512], P('gx', 'gy', 'gz'), may hold values from 0 to 1
- v_start: float32 [8, 256, 512], P('gx', 'gy', 'gz'), may hold values from 0 to 1
- w_start: float32 [8, 256, 512], P('gx', 'gy', 'gz'), may hold values from 0 to 1
- conduct: float32 [8, 256, 512], P('gx', 'gy', 'gz'), may hold values from 0.02 to 0.14
- direction: float32 [8, 256, 512], P('gx', 'gy', 'gz'), may hold values from -2.4 to 2.4
- obs_weight: float32 [8, 256, 512], P('gx', 'gy', 'gz'), may hold values from 0.25 to 12, as said below
- tissue: int32 [8, 256, 512], P('gx', 'gy', 'gz'), may hold values from 0 to 2
- stim_x: int32 [16], replicated, may hold values from 0 to 7
- stim_y: int32 [16], replicated, may hold values from 0 to 255
- stim_z: int32 [16], replicated, may hold values from 0 to 511
- stim_step: int32 [16], replicated, may hold values from 0 to 3
Outputs:
- hess_vec: float32 [8, 256, 512], P('gx', 'gy', 'gz')
- curvature: float32 [], replicated
Inputs may be any that keep to these rules, and one draw needn't show every extreme that they name: 0 marks scar, 1 healthy tissue, 2 tissue with fibers along the first dimension. `obs_weight`: positive weights.
All inputs are finite; a program needn't handle non-finite values.
Results may differ from a plain program's by a relative error of at most 0.0003.
Values sent between devices are 32-bit elements; how exact they have to be, the bound alone decides.
A program may use at most 64 MiB of HBM per device.

v0:
```python
from functools import partial

import jax
import jax.numpy as jnp
from jax import lax
from jax.sharding import PartitionSpec as P

STEPS = 4


time_step = 0.25
u_crit = 0.13
u_gate = 0.04
switch_width = 0.05
tau_fast = 0.4
tau_open = 12.5
tau_repol = 33.33
tau_slow = 15.0
k_slow = 10.0
u_slow = 0.85
tau_vplus = 3.33
tau_vminus_one = 19.6
tau_vminus_two = 1000.0
tau_wplus = 667.0
tau_wminus = 11.0
stim_amp = 2.0
tv_weight = 0.05
tv_smooth = 0.02


def extended(x, sides, width):
    for axis, dim in sides:
        size, length = (lax.axis_size(axis), x.shape[dim])
        up = [(i, (i + 1) % size) for i in range(size - 1)]
        down = [(j, i) for i, j in up]
        last = lax.slice_in_dim(x, length - width, length, axis=dim)
        leading = lax.slice_in_dim(x, 0, width, axis=dim)
        before = lax.ppermute(last, axis, up)
        after = lax.ppermute(leading, axis, down)
        x = jnp.concatenate([before, x, after], axis=dim)
    return x


def switch(value):
    return 0.5 * (1.0 + jnp.tanh(value / switch_width))


def react(u_cell, v_gate, w_gate, stim_count):
    opened = switch(u_cell - u_crit)
    partly = switch(u_cell - u_gate)
    fast_in = -v_gate * opened * (1.0 - u_cell) * (u_cell - u_crit) / tau_fast
    slow_out = u_cell * (1.0 - opened) / tau_open + opened / tau_repol
    slow_in = -w_gate * (1.0 + jnp.tanh(k_slow * (u_cell - u_slow))) / (2.0 * tau_slow)
    u_next = u_cell + time_step * (stim_amp * stim_count - (fast_in + slow_out + slow_in))
    closed = 1.0 - opened
    v_rate = opened / tau_vplus + closed / (
        partly * tau_vminus_one + (1.0 - partly) * tau_vminus_two
    )
    w_rate = opened / tau_wplus + closed / tau_wminus
    v_next = closed + (v_gate - closed) * jnp.exp(-time_step * v_rate)
    w_next = closed + (w_gate - closed) * jnp.exp(-time_step * w_rate)
    return (u_next, v_next, w_next)


def kappas(tissue):
    scar = (tissue == 0).astype(jnp.float32)
    healthy = (tissue == 1).astype(jnp.float32)
    fiber = (tissue == 2).astype(jnp.float32)
    return (0.1 * scar + healthy + 1.5 * fiber, 0.1 * scar + healthy + 0.75 * fiber)


def shifted(padded, axis, offset):
    index = [
        slice(1, padded.shape[0] - 1),
        slice(1, padded.shape[1] - 1),
        slice(1, padded.shape[2] - 1),
    ]
    index[axis] = slice(1 + offset, padded.shape[axis] - 1 + offset)
    return padded[tuple(index)]


def crop(array, width):
    return array[
        width : array.shape[0] - width,
        width : array.shape[1] - width,
        width : array.shape[2] - width,
    ]


def spread(along_c, across_c, live, values):
    centre = shifted(values, 0, 0)
    result = jnp.zeros(centre.shape, jnp.float32)
    for axis in range(3):
        coeff = along_c if axis == 0 else across_c
        own = shifted(coeff, axis, 0)
        for offset in (1, -1):
            face = 0.5 * (own + shifted(coeff, axis, offset)) * shifted(live, axis, offset)
            result = result + face * (shifted(values, axis, offset) - centre)
    return result


def sigma_term(along, across, live, u_pad, adj_pad):
    u_centre = shifted(u_pad, 0, 0)
    a_centre = shifted(adj_pad, 0, 0)
    parts = []
    for axis in range(3):
        part_sum = jnp.zeros(u_centre.shape, jnp.float32)
        for offset in (1, -1):
            part_sum = part_sum + 0.5 * (shifted(u_pad, axis, offset) - u_centre) * (
                a_centre - shifted(adj_pad, axis, offset)
            ) * shifted(live, axis, offset)
        parts.append(part_sum)
    return along * parts[0] + across * (parts[1] + parts[2])


def forward_diff(padded, live, axis):
    lower = [slice(0, -1), slice(0, -1), slice(0, -1)]
    upper = [slice(0, -1), slice(0, -1), slice(0, -1)]
    upper[axis] = slice(1, None)
    return (padded[tuple(upper)] - padded[tuple(lower)]) * live[tuple(upper)] * live[tuple(lower)]


def tv_apply(sig_pad, dir_pad, live):
    diffs = [forward_diff(sig_pad, live, axis) for axis in range(3)]
    weight = 1.0 / jnp.sqrt(
        diffs[0] * diffs[0] + diffs[1] * diffs[1] + diffs[2] * diffs[2] + tv_smooth * tv_smooth
    )
    result = None
    for axis in range(3):
        flux = weight * forward_diff(dir_pad, live, axis)
        here = flux[1:, 1:, 1:]
        index = [slice(1, None), slice(1, None), slice(1, None)]
        index[axis] = slice(0, -1)
        term = flux[tuple(index)] - here
        result = term if result is None else result + term
    return result


def stimulus(step, xs_coord, ys_coord, zs_coord, stim_x, stim_y, stim_z, stim_step):
    active = (stim_step == step).astype(jnp.float32)
    near_x = (jnp.abs(xs_coord[None, :] - stim_x[:, None]) <= 1).astype(jnp.float32) * active[
        :, None
    ]
    near_y = (jnp.abs(ys_coord[None, :] - stim_y[:, None]) <= 1).astype(jnp.float32)
    near_z = (jnp.abs(zs_coord[None, :] - stim_z[:, None]) <= 1).astype(jnp.float32)
    return jnp.einsum("si,sj,sk->ijk", near_x, near_y, near_z, precision=lax.Precision.HIGHEST)


def advance(u_pad, du_pad, v_gate, w_gate, dv_gate, dw_gate, coeffs, live, stim_now):
    c_along, c_across, d_along, d_across = coeffs
    primal, tangent = jax.jvp(
        partial(react, stim_count=stim_now),
        (crop(u_pad, 1), v_gate, w_gate),
        (crop(du_pad, 1), dv_gate, dw_gate),
    )
    u_next = primal[0] + spread(c_along, c_across, live, u_pad)
    du_next = (
        tangent[0]
        + spread(c_along, c_across, live, du_pad)
        + spread(d_along, d_across, live, u_pad)
    )
    return (u_next, primal[1], primal[2], du_next, tangent[1], tangent[2])


def shards(
    u_start,
    v_start,
    w_start,
    conduct,
    direction,
    obs_weight,
    tissue,
    stim_x,
    stim_y,
    stim_z,
    stim_step,
):
    shapes = u_start.shape
    anchor = (
        lax.axis_index("gx") * shapes[0],
        lax.axis_index("gy") * shapes[1],
        lax.axis_index("gz") * shapes[2],
    )
    limits = (
        shapes[0] * lax.axis_size("gx"),
        shapes[1] * lax.axis_size("gy"),
        shapes[2] * lax.axis_size("gz"),
    )
    voxels = limits[0] * limits[1] * limits[2]
    along, across = kappas(tissue)

    def grid_at(width):
        vectors = []
        flags = []
        for axis in range(3):
            coord = anchor[axis] - width + jnp.arange(shapes[axis] + 2 * width, dtype=jnp.int32)
            vectors.append(coord)
            flags.append(((coord >= 0) & (coord < limits[axis])).astype(jnp.float32))
        live = flags[0][:, None, None] * flags[1][None, :, None] * flags[2][None, None, :]
        return (vectors, live)

    inner_vectors, unused_live = grid_at(0)
    outer_vectors, live_one = grid_at(1)
    u_saved, v_saved, w_saved, du_saved = ([], [], [], [])
    static = extended(
        jnp.stack([conduct, direction, along, across, u_start]),
        (("gx", 1), ("gy", 2), ("gz", 3)),
        1,
    )
    sig_pad, dir_pad, along_pad, across_pad, u_pad = (
        static[0],
        static[1],
        static[2],
        static[3],
        static[4],
    )
    coeffs = (along_pad * sig_pad, across_pad * sig_pad, along_pad * dir_pad, across_pad * dir_pad)
    du_pad = jnp.zeros(u_pad.shape, jnp.float32)
    v_gate, w_gate = (v_start, w_start)
    dv_gate = jnp.zeros(shapes, jnp.float32)
    dw_gate = jnp.zeros(shapes, jnp.float32)
    for step in range(STEPS):
        u_saved.append(u_pad)
        v_saved.append(v_gate)
        w_saved.append(w_gate)
        u_cell, v_gate, w_gate, du_cell, dv_gate, dw_gate = advance(
            u_pad,
            du_pad,
            v_gate,
            w_gate,
            dv_gate,
            dw_gate,
            coeffs,
            live_one,
            stimulus(
                step,
                inner_vectors[0],
                inner_vectors[1],
                inner_vectors[2],
                stim_x,
                stim_y,
                stim_z,
                stim_step,
            ),
        )
        du_saved.append(du_cell)
        if step + 1 < STEPS:
            moved = extended(jnp.stack([u_cell, du_cell]), (("gx", 1), ("gy", 2), ("gz", 3)), 1)
            u_pad, du_pad = (moved[0], moved[1])
    c_along, c_across = (coeffs[0], coeffs[1])
    adj_u = obs_weight * du_saved[-1]
    adj_v = jnp.zeros(shapes, jnp.float32)
    adj_w = jnp.zeros(shapes, jnp.float32)
    gradient = jnp.zeros(shapes, jnp.float32)
    zero_stim = jnp.zeros(shapes, jnp.float32)
    for step in reversed(range(STEPS)):
        adj_pad = extended(adj_u, (("gx", 0), ("gy", 1), ("gz", 2)), 1)
        gradient = gradient + sigma_term(along, across, live_one, u_saved[step], adj_pad)
        if step > 0:
            _, pull = jax.vjp(
                partial(react, stim_count=zero_stim),
                crop(u_saved[step], 1),
                v_saved[step],
                w_saved[step],
            )
            back_u, back_v, back_w = pull((adj_u, adj_v, adj_w))
            adj_u = (
                back_u
                + spread(c_along, c_across, live_one, adj_pad)
                + obs_weight * du_saved[step - 1]
            )
            adj_v, adj_w = (back_v, back_w)
    prior = tv_apply(sig_pad, dir_pad, live_one)
    weight_sum, misfit_part, prior_part = lax.psum(
        (jnp.sum(obs_weight), jnp.sum(direction * gradient), jnp.sum(direction * prior)),
        ("gx", "gy", "gz"),
    )
    factor = voxels / weight_sum
    hess_vec = gradient * factor + tv_weight * prior
    curvature = misfit_part * factor + tv_weight * prior_part
    return (hess_vec, curvature)


def solution(mesh):
    in_specs = (
        P("gx", "gy", "gz"),
        P("gx", "gy", "gz"),
        P("gx", "gy", "gz"),
        P("gx", "gy", "gz"),
        P("gx", "gy", "gz"),
        P("gx", "gy", "gz"),
        P("gx", "gy", "gz"),
        P(),
        P(),
        P(),
        P(),
    )
    out_specs = (P("gx", "gy", "gz"), P())
    return jax.shard_map(shards, mesh=mesh, in_specs=in_specs, out_specs=out_specs, check_vma=False)
```

profile of v0, /device:TPU:0, one launch (start us, length us, event | category | flops | bytes accessed | tf_op | source)
XLA Modules:
  0.0 284.1 jit_solution(11126701379574061567)
XLA Ops:
  5.0 4.9 %collective-permute-start = (f32[5,1,64,128]{3,2,1,0:T(8,128)S(1)}, f32[5,1,64,128]{3,2,1,0:T(8,128)S(1)}, u32[]{:S(2)}, u32[]{:S(2)}) collective-permute-start(f32[5,1,64,128]{3,2,1,0:T(8,128)S(1)} %get-tuple-element.49), channel_id=1, source_target_pairs={{0,16},{1,17},{2,18},{3,19},{4,20},{5,21},{6,22},{7,23},{8,24},{9,... | collective-permute-start | bytes 491528 | tf_op jit(solution)/shard_map/ppermute | solution.py:38
  14.7 4.9 %collective-permute-start.2 = (f32[5,6,1,128]{3,2,1,0:T(1,128)S(1)}, f32[5,6,1,128]{3,2,1,0:T(1,128)S(1)}, u32[]{:S(2)}, u32[]{:S(2)}) collective-permute-start(f32[5,6,1,128]{3,2,1,0:T(1,128)S(1)} %get-tuple-element.41), channel_id=1, source_target_pairs={{0,4},{4,8},{8,12},{1,5},{5,9},{9,13},{2,6},{6,10},{10,14},{3,7},{... | collective-permute-start | bytes 46088 | tf_op jit(solution)/shard_map/ppermute | solution.py:38
  33.1 4.5 %collective-permute-start.6 = (f32[2,1,64,128]{3,2,1,0:T(8,128)S(1)}, f32[2,1,64,128]{3,2,1,0:T(8,128)S(1)}, u32[]{:S(2)}, u32[]{:S(2)}) collective-permute-start(f32[2,1,64,128]{3,2,1,0:T(8,128)S(1)} %get-tuple-element.67), channel_id=1, source_target_pairs={{0,16},{1,17},{2,18},{3,19},{4,20},{5,21},{6,22},{7,23},{8,24},{9,... | collective-permute-start | bytes 196616 | tf_op jit(solution)/shard_map/ppermute | solution.py:38
  41.0 4.8 %collective-permute-start.8 = (f32[2,6,1,128]{3,2,1,0:T(1,128)S(1)}, f32[2,6,1,128]{3,2,1,0:T(1,128)S(1)}, u32[]{:S(2)}, u32[]{:S(2)}) collective-permute-start(f32[2,6,1,128]{3,2,1,0:T(1,128)S(1)} %get-tuple-element.61), channel_id=1, source_target_pairs={{0,4},{4,8},{8,12},{1,5},{5,9},{9,13},{2,6},{6,10},{10,14},{3,7},{... | collective-permute-start | bytes 18440 | tf_op jit(solution)/shard_map/ppermute | solution.py:38
  56.7 4.5 %collective-permute-start.12 = (f32[2,1,64,128]{3,2,1,0:T(8,128)S(1)}, f32[2,1,64,128]{3,2,1,0:T(8,128)S(1)}, u32[]{:S(2)}, u32[]{:S(2)}) collective-permute-start(f32[2,1,64,128]{3,2,1,0:T(8,128)S(1)} %get-tuple-element.65), channel_id=1, source_target_pairs={{0,16},{1,17},{2,18},{3,19},{4,20},{5,21},{6,22},{7,23},{8,24},{9,... | collective-permute-start | bytes 196616 | tf_op jit(solution)/shard_map/ppermute | solution.py:38
  64.5 4.9 %collective-permute-start.14 = (f32[2,6,1,128]{3,2,1,0:T(1,128)S(1)}, f32[2,6,1,128]{3,2,1,0:T(1,128)S(1)}, u32[]{:S(2)}, u32[]{:S(2)}) collective-permute-start(f32[2,6,1,128]{3,2,1,0:T(1,128)S(1)} %get-tuple-element.59), channel_id=1, source_target_pairs={{0,4},{4,8},{8,12},{1,5},{5,9},{9,13},{2,6},{6,10},{10,14},{3,7},{... | collective-permute-start | bytes 18440 | tf_op jit(solution)/shard_map/ppermute | solution.py:38
  72.3 7.5 %collective-permute-start.16 = (f32[2,6,66,1]{3,2,1,0:T(8,128)S(1)}, f32[2,6,66,1]{3,2,1,0:T(8,128)S(1)}, u32[]{:S(2)}, u32[]{:S(2)}) collective-permute-start(f32[2,6,66,1]{3,2,1,0:T(8,128)S(1)} %get-tuple-element.53), channel_id=1, source_target_pairs={{0,1},{1,2},{2,3},{4,5},{5,6},{6,7},{8,9},{9,10},{10,11},{12,13},{... | collective-permute-start | bytes 9512 | tf_op jit(solution)/shard_map/ppermute | solution.py:38
  85.2 4.5 %collective-permute-start.18 = (f32[2,1,64,128]{3,2,1,0:T(8,128)S(1)}, f32[2,1,64,128]{3,2,1,0:T(8,128)S(1)}, u32[]{:S(2)}, u32[]{:S(2)}) collective-permute-start(f32[2,1,64,128]{3,2,1,0:T(8,128)S(1)} %get-tuple-element.63), channel_id=1, source_target_pairs={{0,16},{1,17},{2,18},{3,19},{4,20},{5,21},{6,22},{7,23},{8,24},{9,... | collective-permute-start | bytes 196616 | tf_op jit(solution)/shard_map/ppermute | solution.py:38
  93.0 4.5 %collective-permute-start.20 = (f32[2,6,1,128]{3,2,1,0:T(1,128)S(1)}, f32[2,6,1,128]{3,2,1,0:T(1,128)S(1)}, u32[]{:S(2)}, u32[]{:S(2)}) collective-permute-start(f32[2,6,1,128]{3,2,1,0:T(1,128)S(1)} %get-tuple-element.57), channel_id=1, source_target_pairs={{0,4},{4,8},{8,12},{1,5},{5,9},{9,13},{2,6},{6,10},{10,14},{3,7},{... | collective-permute-start | bytes 18440 | tf_op jit(solution)/shard_map/ppermute | solution.py:38
  100.4 9.3 %collective-permute-start.22 = (f32[2,6,66,1]{3,2,1,0:T(8,128)S(1)}, f32[2,6,66,1]{3,2,1,0:T(8,128)S(1)}, u32[]{:S(2)}, u32[]{:S(2)}) collective-permute-start(f32[2,6,66,1]{3,2,1,0:T(8,128)S(1)} %get-tuple-element.51), channel_id=1, source_target_pairs={{0,1},{1,2},{2,3},{4,5},{5,6},{6,7},{8,9},{9,10},{10,11},{12,13},{... | collective-permute-start | bytes 9512 | tf_op jit(solution)/shard_map/ppermute | solution.py:38
  115.3 4.5 %collective-permute-start.25 = (f32[1,64,128]{2,1,0:T(8,128)S(1)}, f32[1,64,128]{2,1,0:T(8,128)S(1)}, u32[]{:S(2)}, u32[]{:S(2)}) collective-permute-start(f32[1,64,128]{2,1,0:T(8,128)S(1)} %get-tuple-element.91), channel_id=1, source_target_pairs={{0,16},{1,17},{2,18},{3,19},{4,20},{5,21},{6,22},{7,23},{8,24},{9,... | collective-permute-start | bytes 98312 | tf_op jit(solution)/shard_map/ppermute | solution.py:38
  126.7 4.2 %collective-permute-done.26 = f32[6,1,128]{2,1,0:T(1,128)S(1)} collective-permute-done((f32[6,1,128]{2,1,0:T(1,128)S(1)}, f32[6,1,128]{2,1,0:T(1,128)S(1)}, u32[]{:S(2)}, u32[]{:S(2)}) %collective-permute-start.26) | collective-permute-done | bytes 3104 | tf_op jit(solution)/shard_map/ppermute | solution.py:39
  132.3 8.8 %collective-permute-start.29 = (f32[6,66,1]{2,1,0:T(8,128)S(1)}, f32[6,66,1]{2,1,0:T(8,128)S(1)}, u32[]{:S(2)}, u32[]{:S(2)}) collective-permute-start(f32[6,66,1]{2,1,0:T(8,128)S(1)} %get-tuple-element.75), channel_id=1, source_target_pairs={{0,1},{1,2},{2,3},{4,5},{5,6},{6,7},{8,9},{9,10},{10,11},{12,13},{... | collective-permute-start | bytes 4760 | tf_op jit(solution)/shard_map/ppermute | solution.py:38
  144.7 4.5 %collective-permute-start.31 = (f32[1,64,128]{2,1,0:T(8,128)S(1)}, f32[1,64,128]{2,1,0:T(8,128)S(1)}, u32[]{:S(2)}, u32[]{:S(2)}) collective-permute-start(f32[1,64,128]{2,1,0:T(8,128)S(1)} %get-tuple-element.89), channel_id=1, source_target_pairs={{0,16},{1,17},{2,18},{3,19},{4,20},{5,21},{6,22},{7,23},{8,24},{9,... | collective-permute-start | bytes 98312 | tf_op jit(solution)/shard_map/ppermute | solution.py:38
  156.0 4.2 %collective-permute-done.32 = f32[6,1,128]{2,1,0:T(1,128)S(1)} collective-permute-done((f32[6,1,128]{2,1,0:T(1,128)S(1)}, f32[6,1,128]{2,1,0:T(1,128)S(1)}, u32[]{:S(2)}, u32[]{:S(2)}) %collective-permute-start.32) | collective-permute-done | bytes 3104 | tf_op jit(solution)/shard_map/ppermute | solution.py:39
  161.7 6.8 %collective-permute-start.35 = (f32[6,66,1]{2,1,0:T(8,128)S(1)}, f32[6,66,1]{2,1,0:T(8,128)S(1)}, u32[]{:S(2)}, u32[]{:S(2)}) collective-permute-start(f32[6,66,1]{2,1,0:T(8,128)S(1)} %get-tuple-element.73), channel_id=1, source_target_pairs={{0,1},{1,2},{2,3},{4,5},{5,6},{6,7},{8,9},{9,10},{10,11},{12,13},{... | collective-permute-start | bytes 4760 | tf_op jit(solution)/shard_map/ppermute | solution.py:38
  172.1 4.5 %collective-permute-start.37 = (f32[1,64,128]{2,1,0:T(8,128)S(1)}, f32[1,64,128]{2,1,0:T(8,128)S(1)}, u32[]{:S(2)}, u32[]{:S(2)}) collective-permute-start(f32[1,64,128]{2,1,0:T(8,128)S(1)} %get-tuple-element.87), channel_id=1, source_target_pairs={{0,16},{1,17},{2,18},{3,19},{4,20},{5,21},{6,22},{7,23},{8,24},{9,... | collective-permute-start | bytes 98312 | tf_op jit(solution)/shard_map/ppermute | solution.py:38
  183.2 4.2 %collective-permute-done.38 = f32[6,1,128]{2,1,0:T(1,128)S(1)} collective-permute-done((f32[6,1,128]{2,1,0:T(1,128)S(1)}, f32[6,1,128]{2,1,0:T(1,128)S(1)}, u32[]{:S(2)}, u32[]{:S(2)}) %collective-permute-start.38) | collective-permute-done | bytes 3104 | tf_op jit(solution)/shard_map/ppermute | solution.py:39
  188.8 6.8 %collective-permute-start.41 = (f32[6,66,1]{2,1,0:T(8,128)S(1)}, f32[6,66,1]{2,1,0:T(8,128)S(1)}, u32[]{:S(2)}, u32[]{:S(2)}) collective-permute-start(f32[6,66,1]{2,1,0:T(8,128)S(1)} %get-tuple-element.71), channel_id=1, source_target_pairs={{0,1},{1,2},{2,3},{4,5},{5,6},{6,7},{8,9},{9,10},{10,11},{12,13},{... | collective-permute-start | bytes 4760 | tf_op jit(solution)/shard_map/ppermute | solution.py:38
  201.3 5.7 %collective-permute-start.43 = (f32[1,64,128]{2,1,0:T(8,128)}, f32[1,64,128]{2,1,0:T(8,128)}, u32[]{:S(2)}, u32[]{:S(2)}) collective-permute-start(f32[1,64,128]{2,1,0:T(8,128)} %get-tuple-element.85), channel_id=1, source_target_pairs={{0,16},{1,17},{2,18},{3,19},{4,20},{5,21},{6,22},{7,23},{8,24},{9,... | collective-permute-start | bytes 98312 | tf_op jit(solution)/shard_map/ppermute | solution.py:38
  210.6 4.5 %collective-permute-start.45 = (f32[6,1,128]{2,1,0:T(1,128)S(1)}, f32[6,1,128]{2,1,0:T(1,128)S(1)}, u32[]{:S(2)}, u32[]{:S(2)}) collective-permute-start(f32[6,1,128]{2,1,0:T(1,128)S(1)} %get-tuple-element.77), channel_id=1, source_target_pairs={{0,4},{4,8},{8,12},{1,5},{5,9},{9,13},{2,6},{6,10},{10,14},{3,7},{... | collective-permute-start | bytes 9224 | tf_op jit(solution)/shard_map/ppermute | solution.py:38
  217.4 7.2 %collective-permute-start.47 = (f32[6,66,1]{2,1,0:T(8,128)S(1)}, f32[6,66,1]{2,1,0:T(8,128)S(1)}, u32[]{:S(2)}, u32[]{:S(2)}) collective-permute-start(f32[6,66,1]{2,1,0:T(8,128)S(1)} %get-tuple-element.70), channel_id=1, source_target_pairs={{0,1},{1,2},{2,3},{4,5},{5,6},{6,7},{8,9},{9,10},{10,11},{12,13},{... | collective-permute-start | bytes 4760 | tf_op jit(solution)/shard_map/ppermute | solution.py:38
  226.4 5.1 %collective-permute-done.46 = f32[6,66,1]{2,1,0:T(8,128)S(1)} collective-permute-done((f32[6,66,1]{2,1,0:T(8,128)S(1)}, f32[6,66,1]{2,1,0:T(8,128)S(1)}, u32[]{:S(2)}, u32[]{:S(2)}) %collective-permute-start.46) | collective-permute-done | bytes 1616 | tf_op jit(solution)/shard_map/ppermute | solution.py:39
  235.6 44.7 %all-reduce = (f32[]{:T(128)}, f32[]{:T(128)}, f32[]{:T(128)}) all-reduce(f32[]{:T(128)} %reduce_sum.27, f32[]{:T(128)} %get-tuple-element.3, f32[]{:T(128)} %get-tuple-element.2), channel_id=1, replica_groups=mesh['gx'=2,'gy'=4,'gz'=4] {'gx','gy','gz'}, use_global_device_ids=true, to_apply=%region_1.0 | all-reduce | flops 3 | bytes 24 | tf_op jit(solution)/shard_map/psum | solution.py:274
  (246 shorter events, 108.5 us)
Async XLA Ops:
  3.7 8.5 %collective-permute-start.1 = (f32[5,1,64,128]{3,2,1,0:T(8,128)S(1)}, f32[5,1,64,128]{3,2,1,0:T(8,128)S(1)}, u32[]{:S(2)}, u32[]{:S(2)}) collective-permute-start(f32[5,1,64,128]{3,2,1,0:T(8,128)S(1)} %get-tuple-element.50), channel_id=1, source_target_pairs={{16,0},{17,1},{18,2},{19,3},{20,4},{21,5},{22,6},{23,7},{24,8},{25... | collective-permute-start | bytes 491528 | tf_op jit(solution)/shard_map/ppermute | solution.py:39
  5.0 8.3 %collective-permute-start = (f32[5,1,64,128]{3,2,1,0:T(8,128)S(1)}, f32[5,1,64,128]{3,2,1,0:T(8,128)S(1)}, u32[]{:S(2)}, u32[]{:S(2)}) collective-permute-start(f32[5,1,64,128]{3,2,1,0:T(8,128)S(1)} %get-tuple-element.49), channel_id=1, source_target_pairs={{0,16},{1,17},{2,18},{3,19},{4,20},{5,21},{6,22},{7,23},{8,24},{9,... | collective-permute-start | bytes 491528 | tf_op jit(solution)/shard_map/ppermute | solution.py:38
  13.4 6.3 %collective-permute-start.3 = (f32[5,6,1,128]{3,2,1,0:T(1,128)S(1)}, f32[5,6,1,128]{3,2,1,0:T(1,128)S(1)}, u32[]{:S(2)}, u32[]{:S(2)}) collective-permute-start(f32[5,6,1,128]{3,2,1,0:T(1,128)S(1)} %get-tuple-element.42), channel_id=1, source_target_pairs={{4,0},{8,4},{12,8},{5,1},{9,5},{13,9},{6,2},{10,6},{14,10},{7,3},{... | collective-permute-start | bytes 46088 | tf_op jit(solution)/shard_map/ppermute | solution.py:39
  14.7 6.4 %collective-permute-start.2 = (f32[5,6,1,128]{3,2,1,0:T(1,128)S(1)}, f32[5,6,1,128]{3,2,1,0:T(1,128)S(1)}, u32[]{:S(2)}, u32[]{:S(2)}) collective-permute-start(f32[5,6,1,128]{3,2,1,0:T(1,128)S(1)} %get-tuple-element.41), channel_id=1, source_target_pairs={{0,4},{4,8},{8,12},{1,5},{5,9},{9,13},{2,6},{6,10},{10,14},{3,7},{... | collective-permute-start | bytes 46088 | tf_op jit(solution)/shard_map/ppermute | solution.py:38
  33.1 6.6 %collective-permute-start.6 = (f32[2,1,64,128]{3,2,1,0:T(8,128)S(1)}, f32[2,1,64,128]{3,2,1,0:T(8,128)S(1)}, u32[]{:S(2)}, u32[]{:S(2)}) collective-permute-start(f32[2,1,64,128]{3,2,1,0:T(8,128)S(1)} %get-tuple-element.67), channel_id=1, source_target_pairs={{0,16},{1,17},{2,18},{3,19},{4,20},{5,21},{6,22},{7,23},{8,24},{9,... | collective-permute-start | bytes 196616 | tf_op jit(solution)/shard_map/ppermute | solution.py:38
  56.7 6.4 %collective-permute-start.12 = (f32[2,1,64,128]{3,2,1,0:T(8,128)S(1)}, f32[2,1,64,128]{3,2,1,0:T(8,128)S(1)}, u32[]{:S(2)}, u32[]{:S(2)}) collective-permute-start(f32[2,1,64,128]{3,2,1,0:T(8,128)S(1)} %get-tuple-element.65), channel_id=1, source_target_pairs={{0,16},{1,17},{2,18},{3,19},{4,20},{5,21},{6,22},{7,23},{8,24},{9,... | collective-permute-start | bytes 196616 | tf_op jit(solution)/shard_map/ppermute | solution.py:38
  63.2 6.2 %collective-permute-start.15 = (f32[2,6,1,128]{3,2,1,0:T(1,128)S(1)}, f32[2,6,1,128]{3,2,1,0:T(1,128)S(1)}, u32[]{:S(2)}, u32[]{:S(2)}) collective-permute-start(f32[2,6,1,128]{3,2,1,0:T(1,128)S(1)} %get-tuple-element.60), channel_id=1, source_target_pairs={{4,0},{8,4},{12,8},{5,1},{9,5},{13,9},{6,2},{10,6},{14,10},{7,3},{... | collective-permute-start | bytes 18440 | tf_op jit(solution)/shard_map/ppermute | solution.py:39
  64.5 6.2 %collective-permute-start.14 = (f32[2,6,1,128]{3,2,1,0:T(1,128)S(1)}, f32[2,6,1,128]{3,2,1,0:T(1,128)S(1)}, u32[]{:S(2)}, u32[]{:S(2)}) collective-permute-start(f32[2,6,1,128]{3,2,1,0:T(1,128)S(1)} %get-tuple-element.59), channel_id=1, source_target_pairs={{0,4},{4,8},{8,12},{1,5},{5,9},{9,13},{2,6},{6,10},{10,14},{3,7},{... | collective-permute-start | bytes 18440 | tf_op jit(solution)/shard_map/ppermute | solution.py:38
  71.0 8.8 %collective-permute-start.17 = (f32[2,6,66,1]{3,2,1,0:T(8,128)S(1)}, f32[2,6,66,1]{3,2,1,0:T(8,128)S(1)}, u32[]{:S(2)}, u32[]{:S(2)}) collective-permute-start(f32[2,6,66,1]{3,2,1,0:T(8,128)S(1)} %get-tuple-element.54), channel_id=1, source_target_pairs={{1,0},{2,1},{3,2},{5,4},{6,5},{7,6},{9,8},{10,9},{11,10},{13,12},{... | collective-permute-start | bytes 9512 | tf_op jit(solution)/shard_map/ppermute | solution.py:39
  72.3 8.9 %collective-permute-start.16 = (f32[2,6,66,1]{3,2,1,0:T(8,128)S(1)}, f32[2,6,66,1]{3,2,1,0:T(8,128)S(1)}, u32[]{:S(2)}, u32[]{:S(2)}) collective-permute-start(f32[2,6,66,1]{3,2,1,0:T(8,128)S(1)} %get-tuple-element.53), channel_id=1, source_target_pairs={{0,1},{1,2},{2,3},{4,5},{5,6},{6,7},{8,9},{9,10},{10,11},{12,13},{... | collective-permute-start | bytes 9512 | tf_op jit(solution)/shard_map/ppermute | solution.py:38
  85.2 6.4 %collective-permute-start.18 = (f32[2,1,64,128]{3,2,1,0:T(8,128)S(1)}, f32[2,1,64,128]{3,2,1,0:T(8,128)S(1)}, u32[]{:S(2)}, u32[]{:S(2)}) collective-permute-start(f32[2,1,64,128]{3,2,1,0:T(8,128)S(1)} %get-tuple-element.63), channel_id=1, source_target_pairs={{0,16},{1,17},{2,18},{3,19},{4,20},{5,21},{6,22},{7,23},{8,24},{9,... | collective-permute-start | bytes 196616 | tf_op jit(solution)/shard_map/ppermute | solution.py:38
  99.1 10.6 %collective-permute-start.23 = (f32[2,6,66,1]{3,2,1,0:T(8,128)S(1)}, f32[2,6,66,1]{3,2,1,0:T(8,128)S(1)}, u32[]{:S(2)}, u32[]{:S(2)}) collective-permute-start(f32[2,6,66,1]{3,2,1,0:T(8,128)S(1)} %get-tuple-element.52), channel_id=1, source_target_pairs={{1,0},{2,1},{3,2},{5,4},{6,5},{7,6},{9,8},{10,9},{11,10},{13,12},{... | collective-permute-start | bytes 9512 | tf_op jit(solution)/shard_map/ppermute | solution.py:39
  100.4 10.5 %collective-permute-start.22 = (f32[2,6,66,1]{3,2,1,0:T(8,128)S(1)}, f32[2,6,66,1]{3,2,1,0:T(8,128)S(1)}, u32[]{:S(2)}, u32[]{:S(2)}) collective-permute-start(f32[2,6,66,1]{3,2,1,0:T(8,128)S(1)} %get-tuple-element.51), channel_id=1, source_target_pairs={{0,1},{1,2},{2,3},{4,5},{5,6},{6,7},{8,9},{9,10},{10,11},{12,13},{... | collective-permute-start | bytes 9512 | tf_op jit(solution)/shard_map/ppermute | solution.py:38
  131.0 10.1 %collective-permute-start.28 = (f32[6,66,1]{2,1,0:T(8,128)S(1)}, f32[6,66,1]{2,1,0:T(8,128)S(1)}, u32[]{:S(2)}, u32[]{:S(2)}) collective-permute-start(f32[6,66,1]{2,1,0:T(8,128)S(1)} %get-tuple-element.76), channel_id=1, source_target_pairs={{1,0},{2,1},{3,2},{5,4},{6,5},{7,6},{9,8},{10,9},{11,10},{13,12},{... | collective-permute-start | bytes 4760 | tf_op jit(solution)/shard_map/ppermute | solution.py:39
  132.3 9.9 %collective-permute-start.29 = (f32[6,66,1]{2,1,0:T(8,128)S(1)}, f32[6,66,1]{2,1,0:T(8,128)S(1)}, u32[]{:S(2)}, u32[]{:S(2)}) collective-permute-start(f32[6,66,1]{2,1,0:T(8,128)S(1)} %get-tuple-element.75), channel_id=1, source_target_pairs={{0,1},{1,2},{2,3},{4,5},{5,6},{6,7},{8,9},{9,10},{10,11},{12,13},{... | collective-permute-start | bytes 4760 | tf_op jit(solution)/shard_map/ppermute | solution.py:38
  160.4 8.1 %collective-permute-start.34 = (f32[6,66,1]{2,1,0:T(8,128)S(1)}, f32[6,66,1]{2,1,0:T(8,128)S(1)}, u32[]{:S(2)}, u32[]{:S(2)}) collective-permute-start(f32[6,66,1]{2,1,0:T(8,128)S(1)} %get-tuple-element.74), channel_id=1, source_target_pairs={{1,0},{2,1},{3,2},{5,4},{6,5},{7,6},{9,8},{10,9},{11,10},{13,12},{... | collective-permute-start | bytes 4760 | tf_op jit(solution)/shard_map/ppermute | solution.py:39
  161.7 7.9 %collective-permute-start.35 = (f32[6,66,1]{2,1,0:T(8,128)S(1)}, f32[6,66,1]{2,1,0:T(8,128)S(1)}, u32[]{:S(2)}, u32[]{:S(2)}) collective-permute-start(f32[6,66,1]{2,1,0:T(8,128)S(1)} %get-tuple-element.73), channel_id=1, source_target_pairs={{0,1},{1,2},{2,3},{4,5},{5,6},{6,7},{8,9},{9,10},{10,11},{12,13},{... | collective-permute-start | bytes 4760 | tf_op jit(solution)/shard_map/ppermute | solution.py:38
  187.5 8.1 %collective-permute-start.40 = (f32[6,66,1]{2,1,0:T(8,128)S(1)}, f32[6,66,1]{2,1,0:T(8,128)S(1)}, u32[]{:S(2)}, u32[]{:S(2)}) collective-permute-start(f32[6,66,1]{2,1,0:T(8,128)S(1)} %get-tuple-element.72), channel_id=1, source_target_pairs={{1,0},{2,1},{3,2},{5,4},{6,5},{7,6},{9,8},{10,9},{11,10},{13,12},{... | collective-permute-start | bytes 4760 | tf_op jit(solution)/shard_map/ppermute | solution.py:39
  188.8 7.9 %collective-permute-start.41 = (f32[6,66,1]{2,1,0:T(8,128)S(1)}, f32[6,66,1]{2,1,0:T(8,128)S(1)}, u32[]{:S(2)}, u32[]{:S(2)}) collective-permute-start(f32[6,66,1]{2,1,0:T(8,128)S(1)} %get-tuple-element.71), channel_id=1, source_target_pairs={{0,1},{1,2},{2,3},{4,5},{5,6},{6,7},{8,9},{9,10},{10,11},{12,13},{... | collective-permute-start | bytes 4760 | tf_op jit(solution)/shard_map/ppermute | solution.py:38
  200.0 8.6 %collective-permute-start.42 = (f32[1,64,128]{2,1,0:T(8,128)}, f32[1,64,128]{2,1,0:T(8,128)}, u32[]{:S(2)}, u32[]{:S(2)}) collective-permute-start(f32[1,64,128]{2,1,0:T(8,128)} %get-tuple-element.86), channel_id=1, source_target_pairs={{16,0},{17,1},{18,2},{19,3},{20,4},{21,5},{22,6},{23,7},{24,8},{25... | collective-permute-start | bytes 98312 | tf_op jit(solution)/shard_map/ppermute | solution.py:39
  201.3 7.3 %collective-permute-start.43 = (f32[1,64,128]{2,1,0:T(8,128)}, f32[1,64,128]{2,1,0:T(8,128)}, u32[]{:S(2)}, u32[]{:S(2)}) collective-permute-start(f32[1,64,128]{2,1,0:T(8,128)} %get-tuple-element.85), channel_id=1, source_target_pairs={{0,16},{1,17},{2,18},{3,19},{4,20},{5,21},{6,22},{7,23},{8,24},{9,... | collective-permute-start | bytes 98312 | tf_op jit(solution)/shard_map/ppermute | solution.py:38
  209.3 6.2 %collective-permute-start.44 = (f32[6,1,128]{2,1,0:T(1,128)S(1)}, f32[6,1,128]{2,1,0:T(1,128)S(1)}, u32[]{:S(2)}, u32[]{:S(2)}) collective-permute-start(f32[6,1,128]{2,1,0:T(1,128)S(1)} %get-tuple-element.78), channel_id=1, source_target_pairs={{4,0},{8,4},{12,8},{5,1},{9,5},{13,9},{6,2},{10,6},{14,10},{7,3},{... | collective-permute-start | bytes 9224 | tf_op jit(solution)/shard_map/ppermute | solution.py:39
  217.4 9.0 %collective-permute-start.47 = (f32[6,66,1]{2,1,0:T(8,128)S(1)}, f32[6,66,1]{2,1,0:T(8,128)S(1)}, u32[]{:S(2)}, u32[]{:S(2)}) collective-permute-start(f32[6,66,1]{2,1,0:T(8,128)S(1)} %get-tuple-element.70), channel_id=1, source_target_pairs={{0,1},{1,2},{2,3},{4,5},{5,6},{6,7},{8,9},{9,10},{10,11},{12,13},{... | collective-permute-start | bytes 4760 | tf_op jit(solution)/shard_map/ppermute | solution.py:38
  224.6 6.9 %collective-permute-start.46 = (f32[6,66,1]{2,1,0:T(8,128)S(1)}, f32[6,66,1]{2,1,0:T(8,128)S(1)}, u32[]{:S(2)}, u32[]{:S(2)}) collective-permute-start(f32[6,66,1]{2,1,0:T(8,128)S(1)} %get-tuple-element.69), channel_id=1, source_target_pairs={{1,0},{2,1},{3,2},{5,4},{6,5},{7,6},{9,8},{10,9},{11,10},{13,12},{... | collective-permute-start | bytes 4760 | tf_op jit(solution)/shard_map/ppermute | solution.py:39
  (73 other events, 681.2 us)
where the time goes:
time: 286 us; the launch traced here: 284 us
  starting transfers between devices  157 us (55%)
  waiting for transfers between devices  44.9 us (16%)
  blocking collectives  44.7 us (16%)
  other arithmetic  21.9 us (8%)
  local copies, waits for them, and re-layouts  8.48 us (3%)
  between operations  5.26 us (2%)
    ppermute x24, starting transfers between devices, extended(): before = lax.ppermute(last, axis, up)  126 us
    psum x1, blocking collectives, shards(): lax.psum((jnp.sum(obs_weight), jnp.sum(direction * gradient), jnp.sum(dir...  44.7 us
    ppermute x24, starting transfers between devices, extended(): after = lax.ppermute(leading, axis, down)  31 us
    ppermute x24, waiting for transfers between devices, extended(): before = lax.ppermute(last, axis, up)  24.5 us
    ppermute x24, waiting for transfers between devices, extended(): after = lax.ppermute(leading, axis, down)  20.5 us
  transfers between devices with their start and end apart: 48, of which 27 were waited for; matrix products, arithmetic and copies ran while one was open for 1% of the time, Pallas kernels for 0%

commit v1 on v0

v1 whole, which is shorter than its diff:
```python
from functools import partial

import jax
import jax.numpy as jnp
from jax import lax
from jax.experimental import pallas as pl
from jax.experimental.pallas import tpu as pltpu
from jax.sharding import PartitionSpec as P

STEPS = 4
AXES = ("gx", "gy", "gz")

time_step = 0.25
u_crit = 0.13
u_gate = 0.04
switch_width = 0.05
tau_fast = 0.4
tau_open = 12.5
tau_repol = 33.33
tau_slow = 15.0
k_slow = 10.0
u_slow = 0.85
tau_vplus = 3.33
tau_vminus_one = 19.6
tau_vminus_two = 1000.0
tau_wplus = 667.0
tau_wminus = 11.0
stim_amp = 2.0
tv_weight = 0.05
tv_smooth = 0.02

ROWS = 16
TOP = 8
F32 = jnp.float32


def react(u, v, w, stim, primal, jac_u, jac_gates):
    out = {}
    opened = 0.5 * (1.0 + jnp.tanh((u - u_crit) * (1.0 / switch_width)))
    closed = 1.0 - opened
    slow = jnp.tanh(k_slow * (u - u_slow))
    hump = (1.0 - u) * (u - u_crit)
    uv = (time_step / tau_fast) * opened * hump
    uw = (time_step / (2.0 * tau_slow)) * (1.0 + slow)
    if primal:
        slow_out = u * closed * (1.0 / tau_open) + opened * (1.0 / tau_repol)
        out["u"] = u + (time_step * stim_amp) * stim + v * uv + w * uw - time_step * slow_out
    if jac_u or jac_gates:
        d_open = (2.0 / switch_width) * opened * closed
    if jac_u:
        d_hump = (1.0 + u_crit) - 2.0 * u
        d_fast = v * (1.0 / tau_fast) * (d_open * hump + opened * d_hump)
        d_out = closed * (1.0 / tau_open) + d_open * (1.0 / tau_repol - u * (1.0 / tau_open))
        d_in = w * (k_slow / (2.0 * tau_slow)) * (1.0 - slow * slow)
        out["uu"] = 1.0 + time_step * (d_fast - d_out + d_in)
        out["uv"] = uv
        out["uw"] = uw
    if primal or jac_gates:
        partly = 0.5 * (1.0 + jnp.tanh((u - u_gate) * (1.0 / switch_width)))
        slowness = 1.0 / (partly * tau_vminus_one + (1.0 - partly) * tau_vminus_two)
        keep_v = jnp.exp(-time_step * (opened * (1.0 / tau_vplus) + closed * slowness))
        keep_w = jnp.exp(-time_step * (opened * (1.0 / tau_wplus) + closed * (1.0 / tau_wminus)))
        far_v = (v - closed) * keep_v
        far_w = (w - closed) * keep_w
        out["v"] = closed + far_v
        out["w"] = closed + far_w
        out["vv"] = keep_v
        out["ww"] = keep_w
    if jac_gates:
        d_partly = (2.0 / switch_width) * partly * (1.0 - partly)
        d_rate_v = d_open * (1.0 / tau_vplus - slowness) + closed * d_partly * (
            (tau_vminus_two - tau_vminus_one) * slowness * slowness
        )
        d_rate_w = d_open * (1.0 / tau_wplus - 1.0 / tau_wminus)
        out["vu"] = d_open * (keep_v - 1.0) - time_step * far_v * d_rate_v
        out["wu"] = d_open * (keep_w - 1.0) - time_step * far_w * d_rate_w
    return out


def kernel(
    sizes,
    u_in,
    v_in,
    w_in,
    c_in,
    d_in,
    obs_in,
    tissue_in,
    sx_in,
    sy_in,
    sz_in,
    ss_in,
    hess_out,
    curv_out,
    pot,
    adj,
    kal,
    kac,
    cd,
    face,
    gates,
    dgates,
    bgates,
    jac,
    local,
    stim,
    zdiff,
    grad,
    qx,
    qy,
    qz,
    sums,
    zsend,
    zrecv,
    ysend,
    yrecv,
    red_own,
    red_x,
    red_y,
    red_z,
    send_sem,
    recv_sem,
    rsend_sem,
    rrecv_sem,
):
    X, Y, Z = u_in.shape
    chunks = Y // ROWS
    place = [lax.axis_index(a) for a in AXES]
    has_lo = [p > 0 for p in place]
    has_hi = [p < n - 1 for p, n in zip(place, sizes)]
    lo_flag = [h.astype(F32) for h in has_lo]
    hi_flag = [h.astype(F32) for h in has_hi]

    barrier = pltpu.get_barrier_semaphore()
    for a, n in enumerate(sizes):
        for k in range(1, n):
            pl.semaphore_signal(
                barrier,
                inc=1,
                device_id={AXES[a]: lax.rem(place[a] + k, n)},
                device_id_type=pl.DeviceIdType.MESH,
            )

    lane = lax.broadcasted_iota(jnp.int32, (ROWS, Z), 1)
    row = lax.broadcasted_iota(jnp.int32, (ROWS, Z), 0)
    blk = pl.ds(TOP, Y)

    pending = []
    counter = [0]

    def send(axis, up, src, dst):
        slot = counter[0]
        counter[0] += 1
        step = 1 if up else -1
        n = sizes[axis]
        target = lax.rem(place[axis] + step + n, n)
        copy = pltpu.make_async_remote_copy(
            src_ref=src,
            dst_ref=dst,
            send_sem=send_sem.at[slot],
            recv_sem=recv_sem.at[slot],
            device_id={AXES[axis]: target},
            device_id_type=pl.DeviceIdType.MESH,
        )
        to = has_hi[axis] if up else has_lo[axis]
        fro = has_lo[axis] if up else has_hi[axis]

        @pl.when(to)
        def _():
            copy.start()

        def wait_send():
            @pl.when(to)
            def _():
                copy.wait_send()

        def wait_recv():
            @pl.when(fro)
            def _():
                copy.wait_recv()

        pending.append(wait_send)
        return wait_recv

    def over(body, group=None):
        xs = tuple(range(X)) if group is None else group

        def one(j, carry):
            y0 = pl.multiple_of(j * ROWS, ROWS)
            for x in xs:
                body(x, y0)
            return carry

        lax.fori_loop(0, chunks, one, 0)

    def pack_z(r, which, x, y0, value, first, up=True, down=True):
        k = which * X + x
        rows = pl.ds(y0, ROWS)
        for side, wanted, shift in ((0, up, (k + 1) % Z), (1, down, k)):
            if wanted:
                moved = pltpu.roll(value, shift, 1) if shift else value
                if not first:
                    moved = jnp.where(lane == k, moved, zsend[r, side, rows])
                zsend[r, side, rows] = moved

    def from_z(r, which, x, y0, value, lo=True, hi=True):
        k = which * X + x
        rows = pl.ds(y0, ROWS)
        zm = zp = None
        if lo:
            edge = zrecv[r, 0, rows]
            edge = pltpu.roll(edge, Z - k, 1) if k else edge
            zm = jnp.where(lane == 0, edge, pltpu.roll(value, 1, 1))
        if hi:
            zp = jnp.where(
                lane == Z - 1,
                pltpu.roll(zrecv[r, 1, rows], Z - 1 - k, 1),
                pltpu.roll(value, Z - 1, 1),
            )
        return zm, zp

    def send_y(r, refs, ups, downs):
        for f, ref in enumerate(refs):
            for x in range(X):
                k = f * X + x
                if f < ups:
                    ysend[r, 0, k : k + 1] = ref(x)[TOP + Y - 1 : TOP + Y]
                if f < downs:
                    ysend[r, 1, k : k + 1] = ref(x)[TOP : TOP + 1]
        waits = []
        for side, count, up in ((0, ups, True), (1, downs, False)):
            if count:
                waits.append(send(1, up, ysend.at[r, side], yrecv.at[r, side]))
        return waits

    def unpack_y(r, refs, ups, downs):
        for f, ref in enumerate(refs):
            for x in range(X):
                k = f * X + x
                if f < ups:
                    ref(x)[TOP - 1 : TOP] = yrecv[r, 0, k : k + 1]
                if f < downs:
                    ref(x)[TOP + Y : TOP + Y + 1] = yrecv[r, 1, k : k + 1]

    def send_z(r, up=True, down=True):
        waits = []
        if up:
            waits.append(send(2, True, zsend.at[r, 0], zrecv.at[r, 0]))
        if down:
            waits.append(send(2, False, zsend.at[r, 1], zrecv.at[r, 1]))
        return waits

    outer = (0,) if X == 1 else (0, X - 1)
    inner = tuple(range(1, X - 1))

    def begin(x, y0):
        rows, prow = pl.ds(y0, ROWS), pl.ds(y0 + TOP, ROWS)
        tissue = tissue_in[x, rows]
        u, c, d = u_in[x, rows], c_in[x, rows], d_in[x, rows]
        along = jnp.where(tissue == 0, 0.1, jnp.where(tissue == 1, 1.0, 1.5))
        across = jnp.where(tissue == 0, 0.1, jnp.where(tissue == 1, 1.0, 0.75))
        cx, dx = across * c, across * d
        pot[0, 0, x + 1, prow] = u
        kal[0, x + 1, rows] = along * c
        kal[1, x + 1, rows] = along * d
        kac[0, x, prow] = cx
        kac[1, x, prow] = dx
        cd[0, x + 1, prow] = c
        cd[1, x + 1, prow] = d
        for f, value in enumerate((u, cx, dx, c, d)):
            pack_z(0, f, x, y0, value, x == 0 and f == 0, up=f < 3)

    over(begin, outer)
    pl.semaphore_wait(barrier, sum(n - 1 for n in sizes))
    waits = [
        send(0, True, pot.at[0, 0, X, blk], pot.at[0, 0, 0, blk]),
        send(0, False, pot.at[0, 0, 1, blk], pot.at[0, 0, X + 1, blk]),
        send(0, True, kal.at[:, X], kal.at[:, 0]),
        send(0, False, kal.at[:, 1], kal.at[:, X + 1]),
    ]
    over(begin, inner)
    refs0 = (
        lambda x: pot.at[0, 0, x + 1],
        lambda x: kac.at[0, x],
        lambda x: kac.at[1, x],
        lambda x: cd.at[0, x + 1],
        lambda x: cd.at[1, x + 1],
    )
    waits += send_y(0, refs0, 3, 5)
    waits += send_z(0)
    late = [send(0, False, cd.at[:, 1, blk], cd.at[:, X + 1, blk])]

    def clear(axis, lo, refs):
        @pl.when(jnp.logical_not(has_lo[axis] if lo else has_hi[axis]))
        def _():
            for ref in refs:
                ref[...] = jnp.zeros(ref.shape, F32)

    for lo, p in ((True, 0), (False, X + 1)):
        clear(0, lo, [pot.at[:, :, p], adj.at[:, p], kal.at[:, p]])
    clear(0, False, [cd.at[:, X + 1]])
    clear(0, True, [qx.at[0]])
    for lo, side in ((True, 0), (False, 1)):
        clear(1, lo, [yrecv.at[:, side]])
        clear(2, lo, [zrecv.at[:, side]])

    sx, sy, sz, ss = sx_in[...], sy_in[...], sz_in[...], ss_in[...]
    sites = sx.shape[1]
    ys = place[1] * Y + lax.broadcasted_iota(jnp.int32, (Y, sites), 0)
    zs = place[2] * Z + lax.broadcasted_iota(jnp.int32, (Z, sites), 0)
    near_y = (jnp.abs(ys - sy) <= 1).astype(F32)
    near_z = (jnp.abs(zs - sz) <= 1).astype(F32)
    for t in range(STEPS - 1):
        for x in range(X):
            near_x = jnp.where(ss == t, (jnp.abs(place[0] * X + x - sx) <= 1).astype(F32), 0.0)
            stim[t, x] = lax.dot_general(
                near_y * near_x, near_z, (((1,), (1,)), ((), ())), preferred_element_type=F32
            )

    def local_forward(t):
        last = t == STEPS - 1

        def body(x, y0):
            rows, prow = pl.ds(y0, ROWS), pl.ds(y0 + TOP, ROWS)
            u = pot[t, 0, x + 1, prow]
            if t == 0:
                v, w = v_in[x, rows], w_in[x, rows]
            else:
                v, w = gates[t, 0, x, rows], gates[t, 1, x, rows]
            n = None if last else stim[t, x, rows]
            e = react(u, v, w, n, not last, t > 0, 0 < t < STEPS - 1)
            if not last:
                local[0, x, rows] = e["u"]
                gates[t + 1, 0, x, rows] = e["v"]
                gates[t + 1, 1, x, rows] = e["w"]
            if t > 0:
                du = pot[t, 1, x + 1, prow]
                dlocal = e["uu"] * du
                jac[t, 0, x, rows] = e["uu"]
                if t > 1:
                    dv, dw = dgates[t, 0, x, rows], dgates[t, 1, x, rows]
                    dlocal = dlocal + e["uv"] * dv + e["uw"] * dw
                    jac[t, 1, x, rows] = e["uv"]
                    jac[t, 2, x, rows] = e["uw"]
                local[1, x, rows] = dlocal
                if not last:
                    jac[t, 3, x, rows] = e["vu"]
                    jac[t, 4, x, rows] = e["wu"]
                    new_dv, new_dw = e["vu"] * du, e["wu"] * du
                    if t > 1:
                        jac[t, 5, x, rows] = e["vv"]
                        jac[t, 6, x, rows] = e["ww"]
                        new_dv = new_dv + e["vv"] * dv
                        new_dw = new_dw + e["ww"] * dw
                    dgates[t + 1, 0, x, rows] = new_dv
                    dgates[t + 1, 1, x, rows] = new_dw

        over(body)

    def neighbours(ref, r, which, x, y0):
        value = ref[x + 1, pl.ds(y0 + TOP, ROWS)]
        zm, zp = from_z(r, which, x, y0, value)
        return value, (
            ref[x, pl.ds(y0 + TOP, ROWS)],
            ref[x + 2, pl.ds(y0 + TOP, ROWS)],
            ref[x + 1, pl.ds(y0 + TOP - 1, ROWS)],
            ref[x + 1, pl.ds(y0 + TOP + 1, ROWS)],
            zm,
            zp,
        )

    def face_weights(x, y0):
        rows, prow = pl.ds(y0, ROWS), pl.ds(y0 + TOP, ROWS)
        live = (
            lo_flag[0] if x == 0 else None,
            hi_flag[0] if x == X - 1 else None,
            jnp.where(y0 + row == 0, lo_flag[1], 1.0),
            jnp.where(y0 + row == Y - 1, hi_flag[1], 1.0),
            jnp.where(lane == 0, lo_flag[2], 1.0),
            jnp.where(lane == Z - 1, hi_flag[2], 1.0),
        )
        weights = []
        for f in range(2):
            own = kal[f, x + 1, rows]
            mine = kac[f, x, prow]
            zm, zp = from_z(0, 1 + f, x, y0, mine)
            raw = (
                own + kal[f, x, rows],
                own + kal[f, x + 2, rows],
                mine + kac[f, x, pl.ds(y0 + TOP - 1, ROWS)],
                mine + kac[f, x, pl.ds(y0 + TOP + 1, ROWS)],
                mine + zm,
                mine + zp,
            )
            out = []
            for i in range(6):
                weight = 0.5 * raw[i]
                if live[i] is not None:
                    weight = weight * live[i]
                face[f, i, x, rows] = weight
                out.append(weight)
            weights.append(out)
        return weights

    def dot6(weights, diffs):
        return (weights[0] * diffs[0] + weights[1] * diffs[1]) + (
            (weights[2] * diffs[2] + weights[3] * diffs[3])
            + (weights[4] * diffs[4] + weights[5] * diffs[5])
        )

    def stencil_forward(t):
        last = t == STEPS - 1

        def body(x, y0):
            rows, prow = pl.ds(y0, ROWS), pl.ds(y0 + TOP, ROWS)
            u, around = neighbours(pot.at[t, 0], t, 0, x, y0)
            diffs = [value - u for value in around]
            zdiff[t, 0, x, rows] = diffs[4]
            zdiff[t, 1, x, rows] = diffs[5]
            if t == 0:
                wc, wd = face_weights(x, y0)
            else:
                wc = [face[0, i, x, rows] for i in range(6)]
                wd = [face[1, i, x, rows] for i in range(6)]
            new_du = dot6(wd, diffs)
            if t > 0:
                du, around = neighbours(pot.at[t, 1], t, 1, x, y0)
                new_du = new_du + local[1, x, rows] + dot6(wc, [value - du for value in around])
            obs = obs_in[x, rows]
            weighted = obs * new_du
            if t == 0:
                sums[0, :, :] += obs
            sums[1, :, :] += weighted * new_du
            if last:
                adj[t, x + 1, prow] = weighted
                pack_z(t + 1, 0, x, y0, weighted, x == 0)
            else:
                new_u = local[0, x, rows] + dot6(wc, diffs)
                pot[t + 1, 0, x + 1, prow] = new_u
                pot[t + 1, 1, x + 1, prow] = new_du
                pack_z(t + 1, 0, x, y0, new_u, x == 0)
                pack_z(t + 1, 1, x, y0, new_du, False)

        return body

    def send_x_adj(t):
        return [
            send(0, True, adj.at[t, X, blk], adj.at[t, 0, blk]),
            send(0, False, adj.at[t, 1, blk], adj.at[t, X + 1, blk]),
        ]

    def send_x_pot(t):
        return [
            send(0, True, pot.at[t, :, X, blk], pot.at[t, :, 0, blk]),
            send(0, False, pot.at[t, :, 1, blk], pot.at[t, :, X + 1, blk]),
        ]

    def prior_flux():
        def body(x, y0):
            rows, prow = pl.ds(y0, ROWS), pl.ds(y0 + TOP, ROWS)
            live_y = jnp.where(y0 + row == Y - 1, hi_flag[1], 1.0)
            live_z = jnp.where(lane == Z - 1, hi_flag[2], 1.0)
            steps = []
            for f in range(2):
                own = cd[f, x + 1, prow]
                dx = cd[f, x + 2, prow] - own
                if x == X - 1:
                    dx = dx * hi_flag[0]
                dy = (cd[f, x + 1, pl.ds(y0 + TOP + 1, ROWS)] - own) * live_y
                dz = (from_z(0, 3 + f, x, y0, own, lo=False)[1] - own) * live_z
                steps.append((dx, dy, dz))
            (a, b, c), (p, q, r) = steps
            m = lax.rsqrt(a * a + b * b + c * c + tv_smooth * tv_smooth)
            sums[2, :, :] += m * (p * p + q * q + r * r)
            qx[x + 1, rows] = m * p
            qy[x, prow] = m * q
            flux = m * r
            qz[x, rows] = flux
            pack_z(2 * STEPS, 0, x, y0, flux, x == 0, down=False)

        over(body)

    sums[...] = jnp.zeros(sums.shape, F32)
    refs_u = lambda t: (lambda x: pot.at[t, 0, x + 1], lambda x: pot.at[t, 1, x + 1])
    refs_a = lambda t: (lambda x: adj.at[t, x + 1],)
    refs_q = (lambda x: qy.at[x],)
    qr = 2 * STEPS
    for t in range(STEPS):
        local_forward(t)
        if t == 1:
            for wait in late:
                wait()
            prior_flux()
        for wait in waits:
            wait()
        if t == 0:
            unpack_y(0, refs0, 3, 5)
        else:
            unpack_y(t, refs_u(t), 2, 2)
        body = stencil_forward(t)
        over(body, outer)
        if t == STEPS - 1:
            waits = send_x_adj(t)
            over(body, inner)
            waits += send_y(t + 1, refs_a(t), 1, 1)
            waits += send_z(t + 1)
        else:
            waits = send_x_pot(t + 1)
            over(body, inner)
            waits += send_y(t + 1, refs_u(t + 1), 2, 2)
            waits += send_z(t + 1)
        if t == 1:
            late = [send(0, True, qx.at[X], qx.at[0])]
            late += send_y(qr, refs_q, 1, 0)
            late += send_z(qr, down=False)

    red_bufs = (red_x, red_y, red_z)
    red_base = (0, sizes[0] - 1, sizes[0] + sizes[1] - 2)

    def reduce_start(axis, value):
        n, buf, me = sizes[axis], red_bufs[axis], place[axis]
        red_own[axis] = value
        buf[pl.ds(me, 1)] = value[None]
        waits = []
        for k in range(1, n):
            slot = red_base[axis] + k - 1
            copy = pltpu.make_async_remote_copy(
                src_ref=red_own.at[axis],
                dst_ref=buf.at[me],
                send_sem=rsend_sem.at[slot],
                recv_sem=rrecv_sem.at[slot],
                device_id={AXES[axis]: lax.rem(me + k, n)},
                device_id_type=pl.DeviceIdType.MESH,
            )
            copy.start()
            pending.append(copy.wait_send)
            arrival = pltpu.make_async_remote_copy(
                src_ref=red_own.at[axis],
                dst_ref=buf.at[lax.rem(me + n - k, n)],
                send_sem=rsend_sem.at[slot],
                recv_sem=rrecv_sem.at[slot],
                device_id={AXES[axis]: lax.rem(me + k, n)},
                device_id_type=pl.DeviceIdType.MESH,
            )
            waits.append(arrival.wait_recv)
        return waits

    def reduce_end(axis, waits):
        for wait in waits:
            wait()
        total = red_bufs[axis][0]
        for i in range(1, sizes[axis]):
            total = total + red_bufs[axis][i]
        return total

    part_row = lax.broadcasted_iota(jnp.int32, (8, Z), 0)
    parts = jnp.zeros((8, Z), F32)
    for i in range(3):
        parts = parts + jnp.where(part_row == i, jnp.sum(sums[i], axis=0, keepdims=True), 0.0)
    reduced = reduce_start(2, parts)

    def local_backward(t):
        def body(x, y0):
            rows, prow = pl.ds(y0, ROWS), pl.ds(y0 + TOP, ROWS)
            a = adj[t, x + 1, prow]
            new = jac[t, 0, x, rows] * a
            if t < STEPS - 1:
                b, c = bgates[t + 1, 0, x, rows], bgates[t + 1, 1, x, rows]
                new = new + jac[t, 3, x, rows] * b + jac[t, 4, x, rows] * c
            local[0, x, rows] = new + obs_in[x, rows] * pot[t, 1, x + 1, prow]
            if t > 1:
                new_b = jac[t, 1, x, rows] * a
                new_c = jac[t, 2, x, rows] * a
                if t < STEPS - 1:
                    new_b = new_b + jac[t, 5, x, rows] * b
                    new_c = new_c + jac[t, 6, x, rows] * c
                bgates[t, 0, x, rows] = new_b
                bgates[t, 1, x, rows] = new_c

        over(body)

    def stencil_backward(t):
        def body(x, y0):
            rows, prow = pl.ds(y0, ROWS), pl.ds(y0 + TOP, ROWS)
            a, around = neighbours(adj.at[t], STEPS + (STEPS - 1 - t), 0, x, y0)
            diffs = [value - a for value in around]
            if t > 0:
                wc = [face[0, i, x, rows] for i in range(6)]
                new = local[0, x, rows] + dot6(wc, diffs)
                adj[t - 1, x + 1, prow] = new
                pack_z(STEPS + (STEPS - t), 0, x, y0, new, x == 0)
            ref = pot.at[t, 0]
            u = ref[x + 1, prow]
            px = (ref[x, prow] - u) * diffs[0] * (lo_flag[0] if x == 0 else 1.0)
            px = px + (ref[x + 2, prow] - u) * diffs[1] * (hi_flag[0] if x == X - 1 else 1.0)
            live = [
                jnp.where(y0 + row == 0, lo_flag[1], 1.0),
                jnp.where(y0 + row == Y - 1, hi_flag[1], 1.0),
                jnp.where(lane == 0, lo_flag[2], 1.0),
                jnp.where(lane == Z - 1, hi_flag[2], 1.0),
            ]
            u_diffs = [
                ref[x + 1, pl.ds(y0 + TOP - 1, ROWS)] - u,
                ref[x + 1, pl.ds(y0 + TOP + 1, ROWS)] - u,
                zdiff[t, 0, x, rows],
                zdiff[t, 1, x, rows],
            ]
            pyz = sum(u_diffs[i] * diffs[2 + i] * live[i] for i in range(4))
            tissue = tissue_in[x, rows]
            along = jnp.where(tissue == 0, -0.05, jnp.where(tissue == 1, -0.5, -0.75))
            across = jnp.where(tissue == 0, -0.05, jnp.where(tissue == 1, -0.5, -0.375))
            term = along * px + across * pyz
            if t < STEPS - 1:
                term = term + grad[x, rows]
            grad[x, rows] = term

        return body

    for t in reversed(range(STEPS)):
        r = STEPS + (STEPS - 1 - t)
        if t > 0:
            local_backward(t)
        for wait in waits:
            wait()
        unpack_y(r, refs_a(t), 1, 1)
        body = stencil_backward(t)
        over(body, outer)
        if t > 0:
            waits = send_x_adj(t - 1)
            over(body, inner)
            waits += send_y(r + 1, refs_a(t - 1), 1, 1)
            waits += send_z(r + 1)
            if t == STEPS - 1:
                reduced = reduce_start(1, reduce_end(2, reduced))
            if t == STEPS - 2:
                reduced = reduce_start(0, reduce_end(1, reduced))
        else:
            over(body, inner)
    total = reduce_end(0, reduced)

    for wait in late:
        wait()
    unpack_y(qr, refs_q, 1, 0)
    voxels = float(X * sizes[0]) * float(Y * sizes[1]) * float(Z * sizes[2])
    factor = voxels / jnp.sum(total[0:1], axis=1, keepdims=True)
    misfit = jnp.sum(total[1:2], axis=1, keepdims=True)
    smooth = jnp.sum(total[2:3], axis=1, keepdims=True)
    curv_out[...] = factor * misfit + tv_weight * smooth

    def finish(x, y0):
        rows, prow = pl.ds(y0, ROWS), pl.ds(y0 + TOP, ROWS)
        here = qz[x, rows]
        prior = (
            (qx[x, rows] - qx[x + 1, rows])
            + (qy[x, pl.ds(y0 + TOP - 1, ROWS)] - qy[x, prow])
            + (from_z(qr, 0, x, y0, here, hi=False)[0] - here)
        )
        hess_out[x, rows] = grad[x, rows] * factor + tv_weight * prior

    over(finish)
    for wait in pending:
        wait()


def shards(sizes, *args):
    X, Y, Z = args[0].shape
    dense = lambda *lead: pltpu.VMEM((*lead, Y, Z), F32)
    tall = lambda *lead: pltpu.VMEM((*lead, Y + 2 * TOP, Z), F32)
    lines = sum(n - 1 for n in sizes)
    rounds = 2 * STEPS + 1
    face_rows = -(-5 * X // 8) * 8
    copies = 9 + 6 * (STEPS - 1) + 6 * STEPS + 3
    vmem = pl.BlockSpec(memory_space=pltpu.VMEM)
    stims = [a.reshape(1, a.shape[0]) for a in args[7:]]
    hess, curv = pl.pallas_call(
        partial(kernel, sizes),
        out_shape=(
            jax.ShapeDtypeStruct((X, Y, Z), F32),
            jax.ShapeDtypeStruct((1, 1), F32),
        ),
        in_specs=[vmem] * 11,
        out_specs=(vmem, vmem),
        scratch_shapes=[
            tall(STEPS, 2, X + 2),
            tall(STEPS, X + 2),
            dense(2, X + 2),
            tall(2, X),
            tall(2, X + 2),
            dense(2, 6, X),
            dense(STEPS, 2, X),
            dense(STEPS, 2, X),
            dense(STEPS, 2, X),
            dense(STEPS, 7, X),
            dense(2, X),
            dense(STEPS - 1, X),
            dense(STEPS, 2, X),
            dense(X),
            dense(X + 1),
            tall(X),
            dense(X),
            pltpu.VMEM((3, ROWS, Z), F32),
            dense(rounds, 2),
            dense(rounds, 2),
            pltpu.VMEM((rounds, 2, face_rows, Z), F32),
            pltpu.VMEM((rounds, 2, face_rows, Z), F32),
            pltpu.VMEM((3, 8, Z), F32),
            pltpu.VMEM((sizes[0], 8, Z), F32),
            pltpu.VMEM((sizes[1], 8, Z), F32),
            pltpu.VMEM((sizes[2], 8, Z), F32),
            pltpu.SemaphoreType.DMA((copies,)),
            pltpu.SemaphoreType.DMA((copies,)),
            pltpu.SemaphoreType.DMA((lines,)),
            pltpu.SemaphoreType.DMA((lines,)),
        ],
        compiler_params=pltpu.CompilerParams(
            collective_id=0, has_side_effects=True, vmem_limit_bytes=40 * 1024 * 1024
        ),
    )(*args[:7], *stims)
    return hess, curv.reshape(())


def solution(mesh):
    sizes = tuple(mesh.shape[a] for a in AXES)
    split = P(*AXES)
    return jax.shard_map(
        partial(shards, sizes),
        mesh=mesh,
        in_specs=(split,) * 7 + (P(),) * 4,
        out_specs=(split, P()),
        check_vma=False,
    )
```

time: 286 us -> 51.9 us (0.18)
  starting transfers between devices: 157 us -> 0 us
  waiting for transfers between devices: 44.9 us -> 0 us
  blocking collectives: 44.7 us -> 0 us
  Pallas kernels: 0 us -> 41.5 us
  other arithmetic: 21.9 us -> 0 us
    ppermute x48 -> x0, starting transfers between devices: 157 us -> none  [the longest x24 126 us: extended(): before = lax.ppermute(last, axis, up)]
    ppermute x48 -> x0, waiting for transfers between devices: 44.9 us -> none  [the longest x24 24.5 us: extended(): before = lax.ppermute(last, axis, up)]
    psum x1 -> x0, blocking collectives: 44.7 us -> none  [shards(): lax.psum((jnp.sum(obs_weight), jnp.sum(direction * gradient), jnp.sum(dir...]
    pallas_call x0 -> x1, Pallas kernels: none -> 41.5 us  [shards(): pl.pallas_call(partial(kernel, sizes), out_shape=(jax.ShapeDtypeStruct((X...]
    add x10 -> x0, other arithmetic: 8.19 us -> none  [the longest x3 4.2 us: shards(): back_u + spread(c_along, c_across, live_one, adj_pad)]
    reduce_sum x2 -> x0, other arithmetic: 5.52 us -> none  [the longest x1 3.95 us: shards(): jnp.sum(direction * prior)]
    concatenate x13 -> x0, other arithmetic: 4.32 us -> none  [extended(): x = jnp.concatenate([before, x, after], axis=dim)]
    unnamed x100 -> x23, local copies, waits for them, and re-layouts: 4.31 us -> 7.65 us
  transfers between devices with their start and end apart: 48 -> 0, of which waited for: 27 -> 0; matrix products, arithmetic and copies ran while one was open for 1% -> 0% of each run, Pallas kernels for 0% -> 0%
where the time goes in v1:
time: 51.9 us; the launch traced here: 51.6 us
  Pallas kernels  41.5 us (80%)
  local copies, waits for them, and re-layouts  7.65 us (15%)
  between operations  2.43 us (5%)
    pallas_call x1, Pallas kernels, shards(): pl.pallas_call(partial(kernel, sizes), out_shape=(jax.ShapeDtypeStruct((X...  41.5 us
    unnamed x23, local copies, waits for them, and re-layouts  7.65 us

profile of v1, /device:TPU:0, one launch (start us, length us, event | category | flops | bytes accessed | tf_op | source)
XLA Modules:
  0.0 51.6 jit_solution(14061708999438063735)
XLA Ops:
  0.6 0.0 copy-start.10
  0.6 0.0 copy-start.7
  0.7 0.0 copy-start.8
  0.7 0.0 copy-start.9
  0.7 0.6 %copy-done.10 = s32[16]{0:T(128)S(1)} copy-done((s32[16]{0:T(128)S(1)}, s32[16]{0:T(128)}, u32[]{:S(2)}) %copy-start.10) | copy-done | bytes 88
  1.3 0.0 copy-done.7
  1.3 0.0 copy-done.8
  1.3 0.0 copy-done.9
  1.3 0.0 copy-start
  1.3 0.9 %copy-done = f32[4,64,128]{2,1,0:T(8,128)S(1)} copy-done((f32[4,64,128]{2,1,0:T(8,128)S(1)}, f32[4,64,128]{2,1,0:T(8,128)}, u32[]{:S(2)}) %copy-start) | copy-done | bytes 131096
  2.2 0.0 copy-start.1
  2.2 0.9 %copy-done.1 = f32[4,64,128]{2,1,0:T(8,128)S(1)} copy-done((f32[4,64,128]{2,1,0:T(8,128)S(1)}, f32[4,64,128]{2,1,0:T(8,128)}, u32[]{:S(2)}) %copy-start.1) | copy-done | bytes 131096
  3.1 0.0 copy-start.2
  3.1 0.9 %copy-done.2 = f32[4,64,128]{2,1,0:T(8,128)S(1)} copy-done((f32[4,64,128]{2,1,0:T(8,128)S(1)}, f32[4,64,128]{2,1,0:T(8,128)}, u32[]{:S(2)}) %copy-start.2) | copy-done | bytes 131096
  4.1 0.0 copy-start.3
  4.1 0.9 %copy-done.3 = f32[4,64,128]{2,1,0:T(8,128)S(1)} copy-done((f32[4,64,128]{2,1,0:T(8,128)S(1)}, f32[4,64,128]{2,1,0:T(8,128)}, u32[]{:S(2)}) %copy-start.3) | copy-done | bytes 131096
  5.0 0.0 copy-start.4
  5.0 0.9 %copy-done.4 = f32[4,64,128]{2,1,0:T(8,128)S(1)} copy-done((f32[4,64,128]{2,1,0:T(8,128)S(1)}, f32[4,64,128]{2,1,0:T(8,128)}, u32[]{:S(2)}) %copy-start.4) | copy-done | bytes 131096
  5.9 0.0 copy-start.5
  5.9 0.9 %copy-done.5 = f32[4,64,128]{2,1,0:T(8,128)S(1)} copy-done((f32[4,64,128]{2,1,0:T(8,128)S(1)}, f32[4,64,128]{2,1,0:T(8,128)}, u32[]{:S(2)}) %copy-start.5) | copy-done | bytes 131096
  6.8 0.0 copy-start.6
  6.8 0.9 %copy-done.6 = s32[4,64,128]{2,1,0:T(8,128)S(1)} copy-done((s32[4,64,128]{2,1,0:T(8,128)S(1)}, s32[4,64,128]{2,1,0:T(8,128)}, u32[]{:S(2)}) %copy-start.6) | copy-done | bytes 131096
  7.7 41.5 %shard_map.122 = (f32[4,64,128]{2,1,0:T(8,128)S(1)}, f32[1,1]{1,0:T(1,128)}) custom-call(f32[4,64,128]{2,1,0:T(8,128)S(1)} %copy-done, f32[4,64,128]{2,1,0:T(8,128)S(1)} %copy-done.1, f32[4,64,128]{2,1,0:T(8,128)S(1)} %copy-done.2, f32[4,64,128]{2,1,0:T(8,128)S(1)} %copy-done.3, f32[4,64,128]{2,1,0:T(8,128)S(1)} %copy-done.4, f32[4,64,128]{2,1,0:T(8,128)S(1)} %copy-done.5, ...), custom_call_target="tpu_custom_call" | custom-call | tf_op jit(solution)/shard_map/pallas_call | solution.py:675
  49.2 0.7 %copy.15 = f32[4,64,128]{2,1,0:T(8,128)} copy(f32[4,64,128]{2,1,0:T(8,128)S(1)} %get-tuple-element.8) | data formatting | bytes 262144
Async XLA Ops:
  0.6 0.7 %copy-start.10 = (s32[16]{0:T(128)S(1)}, s32[16]{0:T(128)}, u32[]{:S(2)}) copy-start(s32[16]{0:T(128)} %param.21) | copy-start | bytes 196
  0.6 0.7 %copy-start.7 = (s32[16]{0:T(128)S(1)}, s32[16]{0:T(128)}, u32[]{:S(2)}) copy-start(s32[16]{0:T(128)} %param.18) | copy-start | bytes 196
  0.7 0.7 %copy-start.8 = (s32[16]{0:T(128)S(1)}, s32[16]{0:T(128)}, u32[]{:S(2)}) copy-start(s32[16]{0:T(128)} %param.19) | copy-start | bytes 196
  0.7 0.7 %copy-start.9 = (s32[16]{0:T(128)S(1)}, s32[16]{0:T(128)}, u32[]{:S(2)}) copy-start(s32[16]{0:T(128)} %param.20) | copy-start | bytes 196
  1.3 0.9 %copy-start = (f32[4,64,128]{2,1,0:T(8,128)S(1)}, f32[4,64,128]{2,1,0:T(8,128)}, u32[]{:S(2)}) copy-start(f32[4,64,128]{2,1,0:T(8,128)} %u_in.1) | copy-start | bytes 393220
  2.2 0.9 %copy-start.1 = (f32[4,64,128]{2,1,0:T(8,128)S(1)}, f32[4,64,128]{2,1,0:T(8,128)}, u32[]{:S(2)}) copy-start(f32[4,64,128]{2,1,0:T(8,128)} %v_in.1) | copy-start | bytes 393220
  3.1 0.9 %copy-start.2 = (f32[4,64,128]{2,1,0:T(8,128)S(1)}, f32[4,64,128]{2,1,0:T(8,128)}, u32[]{:S(2)}) copy-start(f32[4,64,128]{2,1,0:T(8,128)} %w_in.1) | copy-start | bytes 393220
  4.1 0.9 %copy-start.3 = (f32[4,64,128]{2,1,0:T(8,128)S(1)}, f32[4,64,128]{2,1,0:T(8,128)}, u32[]{:S(2)}) copy-start(f32[4,64,128]{2,1,0:T(8,128)} %c_in.1) | copy-start | bytes 393220
  5.0 0.9 %copy-start.4 = (f32[4,64,128]{2,1,0:T(8,128)S(1)}, f32[4,64,128]{2,1,0:T(8,128)}, u32[]{:S(2)}) copy-start(f32[4,64,128]{2,1,0:T(8,128)} %d_in.1) | copy-start | bytes 393220
  5.9 0.9 %copy-start.5 = (f32[4,64,128]{2,1,0:T(8,128)S(1)}, f32[4,64,128]{2,1,0:T(8,128)}, u32[]{:S(2)}) copy-start(f32[4,64,128]{2,1,0:T(8,128)} %obs_in.1) | copy-start | bytes 393220
  6.8 0.9 %copy-start.6 = (s32[4,64,128]{2,1,0:T(8,128)S(1)}, s32[4,64,128]{2,1,0:T(8,128)}, u32[]{:S(2)}) copy-start(s32[4,64,128]{2,1,0:T(8,128)} %tissue_in.1) | copy-start | bytes 393220

commit v2 on v1

--- a/solution.py
+++ b/solution.py
@@ -29,7 +29,7 @@
 tv_weight = 0.05
 tv_smooth = 0.02
 
-ROWS = 16
+ROWS = 64
 TOP = 8
 F32 = jnp.float32
 
@@ -79,6 +79,19 @@
 
 def kernel(
     sizes,
+    u_hbm,
+    v_hbm,
+    w_hbm,
+    c_hbm,
+    d_hbm,
+    obs_hbm,
+    tissue_hbm,
+    sx_hbm,
+    sy_hbm,
+    sz_hbm,
+    ss_hbm,
+    hess_out,
+    curv_out,
     u_in,
     v_in,
     w_in,
@@ -90,8 +103,6 @@
     sy_in,
     sz_in,
     ss_in,
-    hess_out,
-    curv_out,
     pot,
     adj,
     kal,
@@ -122,7 +133,24 @@
     recv_sem,
     rsend_sem,
     rrecv_sem,
+    load_sem,
 ):
+    pairs = (
+        (tissue_hbm, tissue_in),
+        (u_hbm, u_in),
+        (c_hbm, c_in),
+        (d_hbm, d_in),
+        (sx_hbm, sx_in),
+        (sy_hbm, sy_in),
+        (sz_hbm, sz_in),
+        (ss_hbm, ss_in),
+        (v_hbm, v_in),
+        (w_hbm, w_in),
+        (obs_hbm, obs_in),
+    )
+    loads = [pltpu.make_async_copy(a, b, load_sem.at[i]) for i, (a, b) in enumerate(pairs)]
+    for load in loads:
+        load.start()
     X, Y, Z = u_in.shape
     chunks = Y // ROWS
     place = [lax.axis_index(a) for a in AXES]
@@ -169,17 +197,12 @@
         def _():
             copy.start()
 
-        def wait_send():
-            @pl.when(to)
-            def _():
-                copy.wait_send()
-
         def wait_recv():
             @pl.when(fro)
             def _():
                 copy.wait_recv()
 
-        pending.append(wait_send)
+        pending.append((axis, up, copy))
         return wait_recv
 
     def over(body, group=None):
@@ -270,6 +293,8 @@
         for f, value in enumerate((u, cx, dx, c, d)):
             pack_z(0, f, x, y0, value, x == 0 and f == 0, up=f < 3)
 
+    for load in loads[:4]:
+        load.wait()
     over(begin, outer)
     pl.semaphore_wait(barrier, sum(n - 1 for n in sizes))
     waits = [
@@ -303,6 +328,9 @@
     for lo, side in ((True, 0), (False, 1)):
         clear(1, lo, [yrecv.at[:, side]])
         clear(2, lo, [zrecv.at[:, side]])
+
+    for load in loads[4:]:
+        load.wait()
 
     sx, sy, sz, ss = sx_in[...], sy_in[...], sz_in[...], ss_in[...]
     sites = sx.shape[1]
@@ -533,7 +561,7 @@
                 device_id_type=pl.DeviceIdType.MESH,
             )
             copy.start()
-            pending.append(copy.wait_send)
+            pending.append((None, None, copy))
             arrival = pltpu.make_async_remote_copy(
                 src_ref=red_own.at[axis],
                 dst_ref=buf.at[lax.rem(me + n - k, n)],
@@ -658,8 +686,19 @@
         hess_out[x, rows] = grad[x, rows] * factor + tv_weight * prior
 
     over(finish)
-    for wait in pending:
-        wait()
+    for axis in (0, 1, 2, None):
+        for up in (True, False):
+            mine = [c for a, b, c in pending if a == axis and (axis is None or b == up)]
+            if axis is None:
+                if up:
+                    for copy in mine:
+                        copy.wait_send()
+                continue
+
+            @pl.when(has_hi[axis] if up else has_lo[axis])
+            def _():
+                for copy in mine:
+                    copy.wait_send()
 
 
 def shards(sizes, *args):
@@ -678,9 +717,10 @@
             jax.ShapeDtypeStruct((X, Y, Z), F32),
             jax.ShapeDtypeStruct((1, 1), F32),
         ),
-        in_specs=[vmem] * 11,
+        in_specs=[pl.BlockSpec(memory_space=pltpu.HBM)] * 11,
         out_specs=(vmem, vmem),
-        scratch_shapes=[
+        scratch_shapes=[pltpu.VMEM(a.shape, a.dtype) for a in (*args[:7], *stims)]
+        + [
             tall(STEPS, 2, X + 2),
             tall(STEPS, X + 2),
             dense(2, X + 2),
@@ -711,9 +751,10 @@
             pltpu.SemaphoreType.DMA((copies,)),
             pltpu.SemaphoreType.DMA((lines,)),
             pltpu.SemaphoreType.DMA((lines,)),
+            pltpu.SemaphoreType.DMA((11,)),
         ],
         compiler_params=pltpu.CompilerParams(
-            collective_id=0, has_side_effects=True, vmem_limit_bytes=40 * 1024 * 1024
+            collective_id=0, has_side_effects=True, vmem_limit_bytes=56 * 1024 * 1024
         ),
     )(*args[:7], *stims)
     return hess, curv.reshape(())

time: 51.9 us -> 40.5 us (0.78)
  local copies, waits for them, and re-layouts: 7.65 us -> 1.57 us
  Pallas kernels: 41.5 us -> 36.3 us
    unnamed x23 -> x1, local copies, waits for them, and re-layouts: 7.65 us -> 1.57 us
    pallas_call x1, Pallas kernels: 41.5 us -> 36.3 us  [shards(): pl.pallas_call(partial(kernel, sizes), out_shape=(jax.ShapeDtypeStruct((X...]
where the time goes in v2:
time: 40.5 us; the launch traced here: 40.4 us
  Pallas kernels  36.3 us (90%)
  between operations  2.45 us (6%)
  local copies, waits for them, and re-layouts  1.57 us (4%)
    pallas_call x1, Pallas kernels, shards(): pl.pallas_call(partial(kernel, sizes), out_shape=(jax.ShapeDtypeStruct((X...  36.3 us
    unnamed x1, local copies, waits for them, and re-layouts  1.57 us

profile of v2, /device:TPU:0, one launch (start us, length us, event | category | flops | bytes accessed | tf_op | source)
XLA Modules:
  0.0 40.4 jit_solution(15591002046986048155)
XLA Ops:
  0.6 36.3 %shard_map.122 = (f32[4,64,128]{2,1,0:T(8,128)}, f32[1,1]{1,0:T(1,128)}) custom-call(f32[4,64,128]{2,1,0:T(8,128)} %u_hbm.1, f32[4,64,128]{2,1,0:T(8,128)} %v_hbm.1, f32[4,64,128]{2,1,0:T(8,128)} %w_hbm.1, f32[4,64,128]{2,1,0:T(8,128)} %c_hbm.1, f32[4,64,128]{2,1,0:T(8,128)} %d_hbm.1, f32[4,64,128]{2,1,0:T(8,128)} %obs_hbm.1, s32[4,64,128]{2,1,0:T(8,128)} %tissue_hbm.1, ...), custom_call_target="tpu_custom_call" | custom-call | tf_op jit(solution)/shard_map/pallas_call | solution.py:714
  37.0 1.6 %copy.15 = f32[4,64,128]{2,1,0:T(8,128)} copy(f32[4,64,128]{2,1,0:T(8,128)} %get-tuple-element.8) | data formatting | bytes 262144

commit v3 on v2

--- a/solution.py
+++ b/solution.py
@@ -253,7 +253,8 @@
         waits = []
         for side, count, up in ((0, ups, True), (1, downs, False)):
             if count:
-                waits.append(send(1, up, ysend.at[r, side], yrecv.at[r, side]))
+                used = pl.ds(0, -(-count * X // 8) * 8)
+                waits.append(send(1, up, ysend.at[r, side, used], yrecv.at[r, side, used]))
         return waits
 
     def unpack_y(r, refs, ups, downs):
@@ -313,7 +314,6 @@
     )
     waits += send_y(0, refs0, 3, 5)
     waits += send_z(0)
-    late = [send(0, False, cd.at[:, 1, blk], cd.at[:, X + 1, blk])]
 
     def clear(axis, lo, refs):
         @pl.when(jnp.logical_not(has_lo[axis] if lo else has_hi[axis]))
@@ -522,6 +522,7 @@
         for wait in waits:
             wait()
         if t == 0:
+            late = [send(0, False, cd.at[:, 1, blk], cd.at[:, X + 1, blk])]
             unpack_y(0, refs0, 3, 5)
         else:
             unpack_y(t, refs_u(t), 2, 2)
@@ -611,12 +612,18 @@
         def body(x, y0):
             rows, prow = pl.ds(y0, ROWS), pl.ds(y0 + TOP, ROWS)
             a, around = neighbours(adj.at[t], STEPS + (STEPS - 1 - t), 0, x, y0)
+            wc = [face[0, i, x, rows] for i in range(6)]
+            new = local[0, x, rows] + dot6(wc, [value - a for value in around])
+            adj[t - 1, x + 1, prow] = new
+            pack_z(STEPS + (STEPS - t), 0, x, y0, new, x == 0)
+
+        return body
+
+    def gradient_of(t):
+        def body(x, y0):
+            rows, prow = pl.ds(y0, ROWS), pl.ds(y0 + TOP, ROWS)
+            a, around = neighbours(adj.at[t], STEPS + (STEPS - 1 - t), 0, x, y0)
             diffs = [value - a for value in around]
-            if t > 0:
-                wc = [face[0, i, x, rows] for i in range(6)]
-                new = local[0, x, rows] + dot6(wc, diffs)
-                adj[t - 1, x + 1, prow] = new
-                pack_z(STEPS + (STEPS - t), 0, x, y0, new, x == 0)
             ref = pot.at[t, 0]
             u = ref[x + 1, prow]
             px = (ref[x, prow] - u) * diffs[0] * (lo_flag[0] if x == 0 else 1.0)
@@ -640,20 +647,45 @@
             term = along * px + across * pyz
             if t < STEPS - 1:
                 term = term + grad[x, rows]
-            grad[x, rows] = term
-
-        return body
+            if t > 0:
+                grad[x, rows] = term
+            else:
+                hess_out[x, rows] = term * factor + hess_out[x, rows]
+
+        over(body)
+
+    def prior_of(x, y0):
+        rows, prow = pl.ds(y0, ROWS), pl.ds(y0 + TOP, ROWS)
+        here = qz[x, rows]
+        hess_out[x, rows] = tv_weight * (
+            (qx[x, rows] - qx[x + 1, rows])
+            + (qy[x, pl.ds(y0 + TOP - 1, ROWS)] - qy[x, prow])
+            + (from_z(qr, 0, x, y0, here, hi=False)[0] - here)
+        )
 
     for t in reversed(range(STEPS)):
         r = STEPS + (STEPS - 1 - t)
         if t > 0:
             local_backward(t)
+        if t < STEPS - 1:
+            gradient_of(t + 1)
+        if t == 0:
+            total = reduce_end(0, reduced)
+            voxels = float(X * sizes[0]) * float(Y * sizes[1]) * float(Z * sizes[2])
+            factor = voxels / jnp.sum(total[0:1], axis=1, keepdims=True)
+            misfit = jnp.sum(total[1:2], axis=1, keepdims=True)
+            smooth = jnp.sum(total[2:3], axis=1, keepdims=True)
+            curv_out[...] = factor * misfit + tv_weight * smooth
+            for wait in late:
+                wait()
+            unpack_y(qr, refs_q, 1, 0)
+            over(prior_of)
         for wait in waits:
             wait()
         unpack_y(r, refs_a(t), 1, 1)
-        body = stencil_backward(t)
-        over(body, outer)
         if t > 0:
+            body = stencil_backward(t)
+            over(body, outer)
             waits = send_x_adj(t - 1)
             over(body, inner)
             waits += send_y(r + 1, refs_a(t - 1), 1, 1)
@@ -663,29 +695,8 @@
             if t == STEPS - 2:
                 reduced = reduce_start(0, reduce_end(1, reduced))
         else:
-            over(body, inner)
-    total = reduce_end(0, reduced)
-
-    for wait in late:
-        wait()
-    unpack_y(qr, refs_q, 1, 0)
-    voxels = float(X * sizes[0]) * float(Y * sizes[1]) * float(Z * sizes[2])
-    factor = voxels / jnp.sum(total[0:1], axis=1, keepdims=True)
-    misfit = jnp.sum(total[1:2], axis=1, keepdims=True)
-    smooth = jnp.sum(total[2:3], axis=1, keepdims=True)
-    curv_out[...] = factor * misfit + tv_weight * smooth
-
-    def finish(x, y0):
-        rows, prow = pl.ds(y0, ROWS), pl.ds(y0 + TOP, ROWS)
-        here = qz[x, rows]
-        prior = (
-            (qx[x, rows] - qx[x + 1, rows])
-            + (qy[x, pl.ds(y0 + TOP - 1, ROWS)] - qy[x, prow])
-            + (from_z(qr, 0, x, y0, here, hi=False)[0] - here)
-        )
-        hess_out[x, rows] = grad[x, rows] * factor + tv_weight * prior
-
-    over(finish)
+            gradient_of(0)
+
     for axis in (0, 1, 2, None):
         for up in (True, False):
             mine = [c for a, b, c in pending if a == axis and (axis is None or b == up)]

time: 40.5 us -> 40.2 us (level)
  no operation moved by 1% of the time
where the time goes in v3:
time: 40.2 us; the launch traced here: 40 us
  Pallas kernels  36 us (90%)
  between operations  2.45 us (6%)
  local copies, waits for them, and re-layouts  1.57 us (4%)
    pallas_call x1, Pallas kernels, shards(): pl.pallas_call(partial(kernel, sizes), out_shape=(jax.ShapeDtypeStruct((X...  36 us
    unnamed x1, local copies, waits for them, and re-layouts  1.57 us

profile of v3, /device:TPU:0, one launch (start us, length us, event | category | flops | bytes accessed | tf_op | source)
XLA Modules:
  0.0 40.0 jit_solution(1941991430446333818)
XLA Ops:
  0.6 36.0 %shard_map.122 = (f32[4,64,128]{2,1,0:T(8,128)}, f32[1,1]{1,0:T(1,128)}) custom-call(f32[4,64,128]{2,1,0:T(8,128)} %u_hbm.1, f32[4,64,128]{2,1,0:T(8,128)} %v_hbm.1, f32[4,64,128]{2,1,0:T(8,128)} %w_hbm.1, f32[4,64,128]{2,1,0:T(8,128)} %c_hbm.1, f32[4,64,128]{2,1,0:T(8,128)} %d_hbm.1, f32[4,64,128]{2,1,0:T(8,128)} %obs_hbm.1, s32[4,64,128]{2,1,0:T(8,128)} %tissue_hbm.1, ...), custom_call_target="tpu_custom_call" | custom-call | tf_op jit(solution)/shard_map/pallas_call | solution.py:725
  36.6 1.6 %copy.15 = f32[4,64,128]{2,1,0:T(8,128)} copy(f32[4,64,128]{2,1,0:T(8,128)} %get-tuple-element.8) | data formatting | bytes 262144
